TPU v7x, 32 devices: a whole 2x2x4 slice. The times are simulated.
32 devices in a mesh: groups: 2 (over y), corr: 16 (over z, x, core).
Axes of the slice: x: 2, y: 2, z: 4, core: 2. Of those that a mesh axis runs over, the one named last changes fastest.
Arguments:
- patterns: bfloat16 [256, 256, 256], P(('groups', 'corr')), parts along dimension 0, may hold values from -6 to 6
- templates: bfloat16 [16, 23040], P('corr'), may hold values from -6 to 6
- sample_pixels: int32 [23040], replicated, may hold values from 0 to 65278, as said below
- fractions: float32 [2, 23040], replicated, may hold values from 0 to 1
Outputs:
- smoothed: bfloat16 [256, 23040], P(('groups', 'corr')), parts along dimension 0
- best: float32 [256], P(('groups', 'corr')), parts along dimension 0
There are 2 independent parts, one for each index of `groups`. A program takes and returns all parts, laid end to end along the dimension named above; an argument that names none is the same for every part. Nothing has to cross between parts.
Inputs may be any that keep to these rules, and one draw needn't show every extreme that they name: `sample_pixels`: each entry is 256 r + c with r and c from 0 to 254.
All inputs are finite; a program needn't handle non-finite values.
Results may differ from a plain program's by a relative error of at most 0.0063.
Values may be sent and summed in bfloat16 or wider, within the bound.
A program may use at most 128 MiB of HBM per device.

v0:
```python
import math

import jax
import jax.numpy as jnp
from jax import lax
from jax.sharding import PartitionSpec as P

RADII = 64
ANGLES = 360
FREQ = 181


kernel_sigma = 1.5
highest = lax.Precision.HIGHEST


def padded_2(block, sides, width):
    for axis, dim in sides:
        count = lax.axis_size(axis)
        forward = [(i, i + 1) for i in range(count - 1)]
        backward = [(target, source) for source, target in forward]
        low = lax.ppermute(
            lax.slice_in_dim(block, block.shape[dim] - width, None, axis=dim), axis, forward
        )
        high = lax.ppermute(lax.slice_in_dim(block, 0, width, axis=dim), axis, backward)
        block = jnp.concatenate([low, block, high], axis=dim)
    return block


def kernels(size):
    offset = (jnp.arange(size)[:, None] - jnp.arange(size)[None, :]).astype(jnp.float32)
    squared = offset * offset
    bell_kernel = jnp.exp(-squared / (2.0 * kernel_sigma**2)) / (
        math.sqrt(2.0 * math.pi) * kernel_sigma
    )
    curve_kernel = (squared / kernel_sigma**4 - 1.0 / kernel_sigma**2) * bell_kernel
    return (bell_kernel.astype(jnp.bfloat16), curve_kernel.astype(jnp.bfloat16))


def dft_tables(angles, freqs):
    angle_ids = jnp.arange(angles, dtype=jnp.int32)
    freq_ids = jnp.arange(freqs, dtype=jnp.int32)
    phase = (angle_ids[:, None] * freq_ids[None, :] % angles).astype(jnp.float32) * (
        2.0 * math.pi / angles
    )
    cosine = jnp.cos(phase)
    sine = jnp.sin(phase)
    forward = jnp.concatenate([cosine, -sine], axis=1)
    edge = (freq_ids == 0) | (2 * freq_ids == angles)
    factor = jnp.where(edge, 1.0, 2.0).astype(jnp.float32) / angles
    inverse = jnp.concatenate([cosine.T * factor[:, None], -sine.T * factor[:, None]], axis=0)
    return (forward, inverse)


def filter_rows(patterns, bell_kernel, curve_kernel, sample_pixels, fractions):
    count, side = (patterns.shape[0], patterns.shape[1])
    left_bell = jnp.einsum(
        "bij,jk->bik", patterns, bell_kernel, preferred_element_type=jnp.float32
    ).astype(jnp.bfloat16)
    left_curve = jnp.einsum(
        "bij,jk->bik", patterns, curve_kernel, preferred_element_type=jnp.float32
    ).astype(jnp.bfloat16)
    filtered = jnp.einsum(
        "ij,bjk->bik", curve_kernel, left_bell, preferred_element_type=jnp.float32
    ) + jnp.einsum("ij,bjk->bik", bell_kernel, left_curve, preferred_element_type=jnp.float32)
    flattened = filtered.reshape(count, side * side)
    across = fractions[0]
    downward = fractions[1]
    polar_rows = (
        (1.0 - across) * (1.0 - downward) * jnp.take(flattened, sample_pixels, axis=1)
        + across * (1.0 - downward) * jnp.take(flattened, sample_pixels + 1, axis=1)
        + (1.0 - across) * downward * jnp.take(flattened, sample_pixels + side, axis=1)
        + across * downward * jnp.take(flattened, sample_pixels + side + 1, axis=1)
    )
    return polar_rows.astype(jnp.bfloat16)


def body(patterns, templates, sample_pixels, fractions):
    bell_kernel, curve_kernel = kernels(patterns.shape[1])
    polar_rows = filter_rows(patterns, bell_kernel, curve_kernel, sample_pixels, fractions)
    padded = padded_2(polar_rows, (("corr", 0),), 1).astype(jnp.float32)
    smoothed = ((padded[:-2] + 2.0 * padded[1:-1] + padded[2:]) * 0.25).astype(jnp.bfloat16)
    smooth_wide = lax.optimization_barrier(smoothed).astype(jnp.float32)
    count = smoothed.shape[0]
    pattern_norm = jnp.sqrt(jnp.sum(smooth_wide * smooth_wide, axis=1) + 1e-06)
    forward, inverse = dft_tables(ANGLES, FREQ)
    pat_spec = jnp.dot(
        smooth_wide.reshape(count * RADII, ANGLES), forward, precision=highest
    ).reshape(count, RADII, 2 * FREQ)
    pattern_stack = jnp.concatenate([pat_spec[:, :, :FREQ], pat_spec[:, :, FREQ:]], axis=1)
    initial = jnp.full((count,), -1e30, jnp.float32)
    widened = lax.all_gather(templates, "corr", axis=0, tiled=True).astype(jnp.float32)
    number = widened.shape[0]
    templ_norm = jnp.sqrt(jnp.sum(widened * widened, axis=1) + 1e-06)
    spectrum = jnp.dot(widened.reshape(number * RADII, ANGLES), forward, precision=highest).reshape(
        number, RADII, 2 * FREQ
    )
    real_part, imag_part, templ_norm = (spectrum[:, :, :FREQ], spectrum[:, :, FREQ:], templ_norm)
    number = real_part.shape[0]
    plus_stack = jnp.concatenate([real_part, imag_part], axis=1)
    minus_stack = jnp.concatenate([imag_part, -real_part], axis=1)
    both_stacks = jnp.concatenate([plus_stack, minus_stack], axis=0)
    cross = jnp.einsum("pck,tck->ptk", pattern_stack, both_stacks, precision=highest)
    stacked = jnp.concatenate([cross[:, :number], cross[:, number:]], axis=2)
    shifted = jnp.einsum("ptk,ks->pts", stacked, inverse, precision=highest)
    scaled = shifted / templ_norm[None, :, None]
    raw_best = jnp.maximum(initial, jnp.max(scaled, axis=(1, 2)))
    best = raw_best * math.sqrt(RADII * ANGLES) / pattern_norm
    return (smoothed, best)


def solution(mesh):
    in_specs = (P(("groups", "corr"), None, None), P("corr", None), P(), P())
    out_specs = (P(("groups", "corr"), None), P(("groups", "corr")))
    return jax.shard_map(body, mesh=mesh, in_specs=in_specs, out_specs=out_specs, check_vma=False)
```

profile of v0, /device:TPU:0, one launch (start us, length us, event | category | flops | bytes accessed | tf_op | source)
XLA Modules:
  0.0 342.9 jit_solution(15863177858636751435)
XLA Ops:
  0.6 0.0 copy-start
  0.6 1.0 compare_select_fusion.3
  1.7 1.6 compare_and_fusion.3
  3.3 0.0 copy-done
  3.3 2.1 fusion.9
  5.4 2.4 add_bitcast_fusion
  7.9 16.3 %copy.59 = f32[8,256,256]{0,2,1:T(8,128)} copy(f32[8,256,256]{1,2,0:T(8,128)S(1)} %add_bitcast_fusion) | data formatting | bytes 4194304 | tf_op jit(solution)/shard_map/reshape | solution.py:66
  24.1 53.6 %gather_fusion = f32[23040,8]{1,0:T(8,128)} fusion(f32[8,65536]{0,1:T(8,128)} %bitcast.62, s32[23552]{0:T(1024)S(1)} %get-tuple-element.32), kind=kCustom, calls=%fused_computation.clone | custom fusion | bytes 1566720 | tf_op jit(solution)/shard_map/jit(_take)/gather | solution.py:70
  77.7 6.4 %copy.42 = f32[23040,8]{0,1:T(8,128)S(1)} copy(f32[23040,8]{1,0:T(8,128)} %gather_fusion) | data formatting | bytes 1474560 | tf_op jit(solution)/shard_map/jit(_take)/gather | solution.py:70
  84.1 53.6 %gather_fusion.1 = f32[23040,8]{1,0:T(8,128)} fusion(f32[8,65536]{0,1:T(8,128)} %bitcast.63, s32[23552]{0:T(1024)S(1)} %get-tuple-element.31), kind=kCustom, calls=%fused_computation.1.clone | custom fusion | bytes 1566720 | tf_op jit(solution)/shard_map/jit(_take)/gather | solution.py:71
  137.7 6.4 %copy.44 = f32[23040,8]{0,1:T(8,128)S(1)} copy(f32[23040,8]{1,0:T(8,128)} %gather_fusion.1) | data formatting | bytes 1474560 | tf_op jit(solution)/shard_map/jit(_take)/gather | solution.py:71
  144.0 0.1 pad_clamp_fusion
  144.1 53.6 %gather_fusion.2 = f32[23040,8]{1,0:T(8,128)} fusion(f32[8,65536]{0,1:T(8,128)} %bitcast.64, s32[23552]{0:T(1024)S(1)} %get-tuple-element.30), kind=kCustom, calls=%fused_computation.2.clone | custom fusion | bytes 1566720 | tf_op jit(solution)/shard_map/jit(_take)/gather | solution.py:72
  197.7 6.4 %copy.46 = f32[23040,8]{0,1:T(8,128)S(1)} copy(f32[23040,8]{1,0:T(8,128)} %gather_fusion.2) | data formatting | bytes 1474560 | tf_op jit(solution)/shard_map/jit(_take)/gather | solution.py:72
  204.0 53.6 %gather_fusion.3 = f32[23040,8]{1,0:T(8,128)} fusion(f32[8,65536]{0,1:T(8,128)} %bitcast.65, s32[23552]{0:T(1024)S(1)} %get-tuple-element.29), kind=kCustom, calls=%fused_computation.3.clone | custom fusion | bytes 1566720 | tf_op jit(solution)/shard_map/jit(_take)/gather | solution.py:73
  257.7 6.4 %copy.48 = f32[23040,8]{0,1:T(8,128)S(1)} copy(f32[23040,8]{1,0:T(8,128)} %gather_fusion.3) | data formatting | bytes 1474560 | tf_op jit(solution)/shard_map/jit(_take)/gather | solution.py:73
  264.1 0.0 copy-done.8
  264.1 1.1 multiply_reduce_fusion.5
  265.2 0.0 copy-done.9
  265.2 0.0 copy-done.10
  265.2 0.0 copy-done.11
  265.2 0.0 copy-start.12
  265.2 0.6 fusion.19
  265.8 0.0 copy-start.4
  265.8 0.1 fusion.82
  265.9 3.0 collective-permute-start
  268.9 1.3 collective-permute-start.1
  270.2 1.5 sine_negate_fusion
  271.8 0.0 copy-start.3
  271.8 0.0 copy-done.4
  271.8 30.0 %all-gather = bf16[16,1,23040]{2,1,0:T(2,128)(2,1)S(1)} all-gather(bf16[1,1,23040]{2,1,0:T(2,128)(2,1)S(1)} %bitcast.67), channel_id=1, replica_groups=mesh['groups'=2,'corr'=16] {'corr'}, dimensions={0}, use_global_device_ids=true | all-gather | bytes 783360 | tf_op jit(solution)/shard_map/all_gather | solution.py:92
  301.9 1.7 multiply_reduce_fusion
  303.6 5.3 %reduce.5 = bf16[16,23040]{1,0:T(8,128)(2,1)} reduce(bf16[16,1,23040]{2,1,0:T(2,128)(2,1)S(1)} %all-gather, bf16[]{:T(256)} %constant.77), dimensions={1}, to_apply=%all-gather.reduce_sub_computation | reduce | bytes 1474562 | tf_op jit(solution)/shard_map/all_gather | solution.py:92
  308.8 3.1 reshape.37
  312.0 3.3 convolution_bitcast_fusion
  315.3 1.8 copy.49
  317.2 1.3 fusion.79
  318.5 2.5 cosine_multiply_fusion
  321.0 2.2 copy.61
  323.2 0.0 copy-start.5
  323.2 1.2 neg.20
  324.5 2.0 copy.62
  326.5 0.0 collective-permute-done
  326.5 0.0 collective-permute-done.1
  326.5 1.3 maximum_convert_fusion
  327.7 0.2 fusion.16
  327.9 0.0 copy-start.2
  328.0 1.8 dot_general.34
  329.7 0.3 multiply_reduce_fusion.1
  330.0 2.1 fusion.24
  332.1 0.2 fusion.80
  332.3 0.1 pad_maximum_fusion
  332.4 0.4 copy.52
  332.8 7.5 %fusion.11 = f32[8,32,181]{1,0,2:T(8,128)S(1)} fusion(f32[8,128,181]{1,0,2:T(8,128)S(1)} %copy.52, f32[16,64,181]{1,0,2:T(8,128)} %neg.20, f32[16,64,181]{1,0,2:T(8,128)} %copy.62, f32[16,64,181]{1,0,2:T(8,128)S(1)} %copy.61), kind=kOutput, calls=%fused_computation.20 | convolution fusion | flops 73396224 | bytes 3150848 | tf_op jit(solution)/shard_map/pck,tck->ptk/dot_general | solution.py:103
  340.4 0.0 copy-start.6
  340.4 0.0 copy-start.7
  340.4 0.0 copy-start.1
  340.4 0.3 fusion.81
  340.7 0.3 copy.53
  341.0 0.3 copy.54
  341.4 0.0 copy-done.6
  341.4 0.1 copy-done.7
  341.5 0.9 fusion.14
  342.4 0.5 rsqrt_multiply_fusion
  (12 shorter events, 0.1 us)
Async XLA Ops:
  0.6 2.7 copy-start
  257.6 6.4 %copy-start.8 = (f32[2,23040]{1,0:T(2,128)S(1)}, f32[2,23040]{1,0:T(2,128)}, u32[]{:S(2)}) copy-start(f32[2,23040]{1,0:T(2,128)} %param.9) | copy-start | bytes 552964
  257.7 7.5 %copy-start.9 = (pred[23040]{0:T(1024)(128)(4,1)S(1)}, pred[23040]{0:T(1024)(128)(4,1)}, u32[]{:S(2)}) copy-start(pred[23040]{0:T(1024)(128)(4,1)} %get-tuple-element.20) | copy-start | bytes 69124
  257.7 7.5 %copy-start.10 = (pred[23040]{0:T(1024)(128)(4,1)S(1)}, pred[23040]{0:T(1024)(128)(4,1)}, u32[]{:S(2)}) copy-start(pred[23040]{0:T(1024)(128)(4,1)} %get-tuple-element.21) | copy-start | bytes 69124
  257.7 7.5 %copy-start.11 = (pred[23040]{0:T(1024)(128)(4,1)S(1)}, pred[23040]{0:T(1024)(128)(4,1)}, u32[]{:S(2)}) copy-start(pred[23040]{0:T(1024)(128)(4,1)} %get-tuple-element.22) | copy-start | bytes 69124
  265.2 6.6 %copy-start.12 = (bf16[1,23040]{1,0:T(2,128)(2,1)S(1)}, bf16[1,23040]{1,0:T(2,128)(2,1)}, u32[]{:S(2)}) copy-start(bf16[1,23040]{1,0:T(2,128)(2,1)} %param.7) | copy-start | bytes 138244
  265.8 6.0 %copy-start.4 = (bf16[8,23040]{1,0:T(8,128)(2,1)}, bf16[8,23040]{1,0:T(8,128)(2,1)S(1)}, u32[]{:S(2)}) copy-start(bf16[8,23040]{1,0:T(8,128)(2,1)S(1)} %fusion.19) | copy-start | bytes 1105924
  265.9 60.5 %collective-permute-start = (bf16[1,23040]{1,0:T(2,128)(2,1)S(1)}, bf16[1,23040]{1,0:T(2,128)(2,1)}, u32[]{:S(2)}, u32[]{:S(2)}) collective-permute-start(bf16[1,23040]{1,0:T(2,128)(2,1)S(1)} %get-tuple-element.17), channel_id=1, source_target_pairs={{0,1},{1,2},{2,3},{3,4},{4,5},{5,6},{6,7},{7,8},{8,9},{9,10},{10,1... | collective-permute-start | bytes 138248 | tf_op jit(solution)/shard_map/ppermute | solution.py:22
  268.9 57.5 %collective-permute-start.1 = (bf16[1,23040]{1,0:T(2,128)(2,1)S(1)}, bf16[1,23040]{1,0:T(2,128)(2,1)}, u32[]{:S(2)}, u32[]{:S(2)}) collective-permute-start(bf16[1,23040]{1,0:T(2,128)(2,1)S(1)} %get-tuple-element.18), channel_id=1, source_target_pairs={{1,0},{2,1},{3,2},{4,3},{5,4},{6,5},{7,6},{8,7},{9,8},{10,9},{11,1... | collective-permute-start | bytes 138248 | tf_op jit(solution)/shard_map/ppermute | solution.py:25
  271.8 40.2 %copy-start.3 = (f32[360,181]{1,0:T(8,128)}, f32[360,181]{1,0:T(8,128)S(1)}, u32[]{:S(2)}) copy-start(f32[360,181]{1,0:T(8,128)S(1)} %get-tuple-element.34) | copy-start | bytes 781924
  323.2 3.2 copy-start.5
  327.9 4.4 %copy-start.2 = (bf16[8,23040]{1,0:T(8,128)(2,1)}, bf16[8,23040]{1,0:T(8,128)(2,1)S(1)}, u32[]{:S(2)}) copy-start(bf16[8,23040]{1,0:T(8,128)(2,1)S(1)} %fusion.16) | copy-start | bytes 1105924
  340.4 1.0 copy-start.6
  340.4 1.1 copy-start.7
  340.4 2.5 copy-start.1
where the time goes:
time: 344 us; the launch traced here: 343 us
  local copies, waits for them, and re-layouts  270 us (78%)
  blocking collectives  30 us (9%)
  other arithmetic  19.1 us (6%)
  matrix products  18.3 us (5%)
  starting transfers between devices  4.29 us (1%)
    gather x2, local copies, waits for them, and re-layouts, filter_rows(): jnp.take(flattened, sample_pixels + side + 1, axis=1)  60 us
    gather x2, local copies, waits for them, and re-layouts, filter_rows(): jnp.take(flattened, sample_pixels + 1, axis=1)  60 us
    gather x2, local copies, waits for them, and re-layouts, filter_rows(): jnp.take(flattened, sample_pixels, axis=1)  59.9 us
    gather x2, local copies, waits for them, and re-layouts, filter_rows(): jnp.take(flattened, sample_pixels + side, axis=1)  59.9 us
    all_gather x1, blocking collectives, body(): lax.all_gather(templates, 'corr', axis=0, tiled=True).astype(jnp.float32)  30 us
    reshape x1, local copies, waits for them, and re-layouts, filter_rows(): flattened = filtered.reshape(count, side * side)  16.3 us
    dot_general x1, matrix products, body(): jnp.einsum('pck,tck->ptk', pattern_stack, both_stacks, precision=highest)  7.51 us
  transfers between devices with their start and end apart: 2, of which 0 were waited for; matrix products, arithmetic and copies ran while one was open for 8% of the time, Pallas kernels for 0%

commit v1 on v0

v1 whole, which is shorter than its diff:
```python
import functools
import math

import jax
import jax.numpy as jnp
import ml_dtypes
import numpy as np
from jax import lax
from jax.experimental import pallas as pl
from jax.experimental.pallas import tpu as pltpu
from jax.sharding import PartitionSpec as P

RADII = 64
ANGLES = 360
FREQ = 181
SIGMA = 1.5
WIDE = 384
HALF = 256
CHUNK = 256
VMEM = pl.BlockSpec(memory_space=pltpu.VMEM)


def filter_tables(size):
    ids = np.arange(size)
    squared = ((ids[:, None] - ids[None, :]) ** 2).astype(np.float32)
    bell = np.exp(-squared / np.float32(2 * SIGMA**2)) / np.float32(math.sqrt(2 * math.pi) * SIGMA)
    curve = (squared / np.float32(SIGMA**4) - np.float32(1 / SIGMA**2)) * bell
    bell, curve = bell.astype(ml_dtypes.bfloat16), curve.astype(ml_dtypes.bfloat16)
    return np.concatenate([bell, curve], axis=1), np.concatenate([curve, bell], axis=1)


def split(table):
    high = table.astype(ml_dtypes.bfloat16)
    low = (table - high.astype(np.float64)).astype(ml_dtypes.bfloat16)
    return np.concatenate([high, low], axis=1)


def dft_tables():
    phase = np.outer(np.arange(ANGLES), np.arange(FREQ)) % ANGLES * (2 * math.pi / ANGLES)
    forward = np.zeros((WIDE, 2 * HALF))
    forward[:ANGLES, :FREQ] = np.cos(phase)
    forward[:ANGLES, HALF : HALF + FREQ] = -np.sin(phase)
    factor = np.full((FREQ, 1), 2.0 / ANGLES)
    factor[0] = factor[FREQ - 1] = 1.0 / ANGLES
    inverse = np.zeros((2 * HALF, WIDE))
    inverse[:FREQ, :ANGLES] = np.cos(phase).T * factor
    inverse[HALF : HALF + FREQ, :ANGLES] = -np.sin(phase).T * factor
    inverse[:, ANGLES:] = inverse[:, :1]
    return split(forward), inverse.astype(np.float32)


def pick(rows, masks):
    for mask in masks:
        rows = [jnp.where(mask, rows[i + 1], rows[i]) for i in range(0, len(rows), 2)]
    return rows[0]


def pick_tree(get, masks, level, at):
    if level == 0:
        return get(at)
    low = pick_tree(get, masks, level - 1, at)
    high = pick_tree(get, masks, level - 1, at + (1 << (level - 1)))
    return jnp.where(masks[level - 1], high, low)


def sample_kernel(pat_ref, first_ref, second_ref, pix_ref, frac_ref, polar_ref, wide_ref, rows_ref):
    count, side = pat_ref.shape[0], pat_ref.shape[1]
    for p in range(count):
        left = jnp.dot(pat_ref[p], first_ref[...], preferred_element_type=jnp.float32)
        left = left.astype(jnp.bfloat16)
        left = jnp.concatenate([left[:, :side], left[:, side:]], axis=0)
        filtered = jnp.dot(second_ref[...], left, preferred_element_type=jnp.float32)
        wide_ref[:, p, :] = filtered
    rows_ref[...] = wide_ref[...].reshape(side * count, side).astype(jnp.bfloat16)

    @pl.loop(0, pix_ref.shape[1] // CHUNK)
    def _(step):
        at = pl.ds(pl.multiple_of(step * CHUNK, CHUNK), CHUNK)
        pixel = pix_ref[:, at]
        across = frac_ref[0:1, at]
        downward = jnp.broadcast_to(frac_ref[1:2, at], (count, CHUNK))
        col = pixel & (side - 1)
        row = jnp.broadcast_to(pixel >> 8, (count, CHUNK))
        ids = lax.broadcasted_iota(jnp.int32, (side, CHUNK), 0)
        weights = jnp.where(
            ids == col, 1.0 - across, jnp.where(ids == col + 1, across, 0.0)
        ).astype(jnp.bfloat16)
        taken = jnp.dot(rows_ref[...], weights, preferred_element_type=jnp.float32)
        bits = side.bit_length() - 2
        even_at, odd_at = (row + 1) >> 1, row >> 1
        even_masks = [(even_at & (1 << b)) != 0 for b in range(bits)]
        odd_masks = [(odd_at & (1 << b)) != 0 for b in range(bits)]

        def row_of(r):
            return taken[r * count : (r + 1) * count]

        even = pick_tree(lambda i: row_of(2 * i), even_masks, bits, 0)
        odd = pick_tree(lambda i: row_of(2 * i + 1), odd_masks, bits, 0)
        is_odd = (row & 1) != 0
        top = jnp.where(is_odd, odd, even)
        bottom = jnp.where(is_odd, even, odd)
        polar = (1.0 - downward) * top + downward * bottom
        polar_ref[:, at] = polar.astype(jnp.bfloat16)


def match_kernel(
    polar_ref, low_ref, high_ref, templ_ref, fwd_ref, inv_ref, smooth_ref, best_ref,
    padded_ref, line_ref, spec_ref, templ_spec_ref, norm_ref, cross_ref,
):
    count, width = polar_ref.shape
    number = templ_ref.shape[0] // RADII
    block = 1152
    ids = lax.broadcasted_iota(jnp.int32, (count, block), 0)
    total = jnp.zeros((count, 128), jnp.float32)
    for start in range(0, width, block):
        at = pl.ds(start, block)
        rows = polar_ref[:, at].astype(jnp.float32)
        low = jnp.broadcast_to(low_ref[:, at].astype(jnp.float32), rows.shape)
        high = jnp.broadcast_to(high_ref[:, at].astype(jnp.float32), rows.shape)
        before = jnp.where(ids == 0, low, pltpu.roll(rows, 1, 0))
        after = jnp.where(ids == count - 1, high, pltpu.roll(rows, count - 1, 0))
        smooth = ((before + 2.0 * rows + after) * 0.25).astype(jnp.bfloat16)
        smooth_ref[:, at] = smooth
        smooth = smooth.astype(jnp.float32)
        padded_ref[:, at] = smooth
        squares = smooth * smooth
        for lane in range(0, block, 128):
            total = total + squares[:, lane : lane + 128]
    pattern_norm = jnp.sqrt(jnp.sum(total, axis=1, keepdims=True) + 1e-06)
    padded_ref[:, width:] = jnp.zeros((count, padded_ref.shape[1] - width), jnp.float32)

    real_lane = lax.broadcasted_iota(jnp.int32, (count, WIDE), 1) < ANGLES
    for r in range(RADII):
        start = r * ANGLES
        base = start // 128 * 128
        window = padded_ref[:, base : base + 512]
        if start > base:
            window = pltpu.roll(window, 512 - (start - base), 1)
        line_ref[r * count : (r + 1) * count, :] = jnp.where(real_lane, window[:, :WIDE], 0.0)

    def spectrum(lines):
        both = jnp.dot(lines, fwd_ref[...], preferred_element_type=jnp.float32)
        return both[:, : 2 * HALF] + both[:, 2 * HALF :]

    spec_ref[...] = spectrum(line_ref[...].astype(jnp.bfloat16))

    @pl.loop(0, number)
    def _(t):
        at = pl.ds(pl.multiple_of(t * RADII, RADII), RADII)
        lines = templ_ref[at, :]
        templ_spec_ref[at, :] = spectrum(lines)
        lines = lines.astype(jnp.float32)
        norm = jnp.sqrt(jnp.sum(lines * lines, keepdims=True) + 1e-06)
        real = [jnp.zeros((count, HALF), jnp.float32)] * 1
        imag = [jnp.zeros((count, HALF), jnp.float32)] * 1
        real, imag = real[0], imag[0]
        for r in range(RADII):
            pat = spec_ref[r * count : (r + 1) * count, :]
            tem = templ_spec_ref[pl.ds(t * RADII + r, 1), :]
            pr, pi, tr, ti = pat[:, :HALF], pat[:, HALF:], tem[:, :HALF], tem[:, HALF:]
            real = real + pr * tr + pi * ti
            imag = imag + pr * ti - pi * tr
        out = pl.ds(pl.multiple_of(t * count, count), count)
        scale = 1.0 / norm
        cross_ref[out, :HALF] = real * scale
        cross_ref[out, HALF:] = imag * scale

    scaled = jnp.dot(
        cross_ref[...], inv_ref[...], precision=lax.Precision.HIGHEST,
        preferred_element_type=jnp.float32,
    )
    top = jnp.max(scaled.reshape(number, count, WIDE), axis=0)
    best = jnp.max(top, axis=1, keepdims=True)
    best = best * math.sqrt(RADII * ANGLES) / pattern_norm
    best_ref[...] = jnp.broadcast_to(best, best_ref.shape)


def body(patterns, templates, pixels, fractions):
    count, side = patterns.shape[0], patterns.shape[1]
    width = pixels.shape[0]
    first, second = filter_tables(side)
    forward, inverse = dft_tables()
    size = lax.axis_size("corr")
    own = templates.reshape(-1, ANGLES)
    own = jnp.pad(own, ((0, 0), (0, WIDE - ANGLES)))
    library = lax.all_gather(own, "corr", axis=0, tiled=True)
    polar = pl.pallas_call(
        sample_kernel,
        out_shape=jax.ShapeDtypeStruct((count, width), jnp.bfloat16),
        in_specs=[VMEM] * 5,
        out_specs=VMEM,
        scratch_shapes=[
            pltpu.VMEM((side, count, side), jnp.float32),
            pltpu.VMEM((side * count, side), jnp.bfloat16),
        ],
        compiler_params=pltpu.CompilerParams(vmem_limit_bytes=40 << 20),
        cost_estimate=pl.CostEstimate(
            flops=2 * count * side * side * width, bytes_accessed=3 << 20, transcendentals=0
        ),
    )(patterns, jnp.asarray(first), jnp.asarray(second), pixels[None], fractions)
    forward_pairs = [(i, i + 1) for i in range(size - 1)]
    backward_pairs = [(i + 1, i) for i in range(size - 1)]
    low = lax.ppermute(polar[count - 1 :], "corr", forward_pairs)
    high = lax.ppermute(polar[:1], "corr", backward_pairs)
    number = library.shape[0] // RADII
    smoothed, best = pl.pallas_call(
        match_kernel,
        out_shape=(
            jax.ShapeDtypeStruct((count, width), jnp.bfloat16),
            jax.ShapeDtypeStruct((count, 128), jnp.float32),
        ),
        in_specs=[VMEM] * 6,
        out_specs=(VMEM, VMEM),
        scratch_shapes=[
            pltpu.VMEM((count, width + 512), jnp.float32),
            pltpu.VMEM((RADII * count, WIDE), jnp.float32),
            pltpu.VMEM((RADII * count, 2 * HALF), jnp.float32),
            pltpu.VMEM((number * RADII, 2 * HALF), jnp.float32),
            pltpu.VMEM((8, 128), jnp.float32),
            pltpu.VMEM((number * count, 2 * HALF), jnp.float32),
        ],
        compiler_params=pltpu.CompilerParams(vmem_limit_bytes=50 << 20),
    )(polar, low, high, library, jnp.asarray(forward), jnp.asarray(inverse))
    return smoothed, best[:, 0]


def solution(mesh):
    in_specs = (P(("groups", "corr"), None, None), P("corr", None), P(), P())
    out_specs = (P(("groups", "corr"), None), P(("groups", "corr")))
    return jax.shard_map(body, mesh=mesh, in_specs=in_specs, out_specs=out_specs, check_vma=False)
```

time: 344 us -> 90 us (0.26)
  local copies, waits for them, and re-layouts: 270 us -> 5.04 us
  Pallas kernels: 0 us -> 54 us
  other arithmetic: 19.1 us -> 0.26 us
  matrix products: 18.3 us -> 0 us
  blocking collectives: 30 us -> 25.3 us
    gather x8 -> x0, local copies, waits for them, and re-layouts: 240 us -> none  [the longest x2 60 us: filter_rows(): jnp.take(flattened, sample_pixels + side + 1, axis=1)]
    pallas_call x0 -> x2, Pallas kernels: none -> 54 us  [the longest x1 43.3 us: body(): pl.pallas_call(sample_kernel, out_shape=jax.ShapeDtypeStruct((count, widt...]
    reshape x2 -> x1, local copies, waits for them, and re-layouts: 19.4 us -> 0.15 us  [body(): own = templates.reshape(-1, ANGLES)]
    dot_general x6 -> x0, matrix products: 18.3 us -> none  [the longest x1 7.51 us: body(): jnp.einsum('pck,tck->ptk', pattern_stack, both_stacks, precision=highest)]
    all_gather x1 -> x0, other arithmetic: 5.29 us -> none  [body(): lax.all_gather(templates, 'corr', axis=0, tiled=True).astype(jnp.float32)]
    all_gather x1, blocking collectives: 30 us -> 25.3 us  [body(): library = lax.all_gather(own, 'corr', axis=0, tiled=True)]
    dot_general x2 -> x0, local copies, waits for them, and re-layouts: 3.62 us -> none  [the longest x1 1.85 us: body(): jnp.dot(widened.reshape(number * RADII, ANGLES), forward, precision=highest)]
    mul x2 -> x0, other arithmetic: 3.55 us -> none  [the longest x1 2.47 us: dft_tables(): cosine.T * factor[:, None]]
  transfers between devices with their start and end apart: 2 -> 2, of which waited for: 0 -> 0; matrix products, arithmetic and copies ran while one was open for 8% -> 0% of each run, Pallas kernels for 0% -> 0%
where the time goes in v1:
time: 90 us; the launch traced here: 89.7 us
  Pallas kernels  54 us (60%)
  blocking collectives  25.3 us (28%)
  local copies, waits for them, and re-layouts  5.04 us (6%)
  starting transfers between devices  4.46 us (5%)
    pallas_call x1, Pallas kernels, body(): pl.pallas_call(sample_kernel, out_shape=jax.ShapeDtypeStruct((count, widt...  43.3 us
    all_gather x1, blocking collectives, body(): library = lax.all_gather(own, 'corr', axis=0, tiled=True)  25.3 us
    pallas_call x1, Pallas kernels, body(): pl.pallas_call(match_kernel, out_shape=(jax.ShapeDtypeStruct((count, widt...  10.7 us
    unnamed x14, local copies, waits for them, and re-layouts  3.14 us
    ppermute x1, starting transfers between devices, body(): low = lax.ppermute(polar[count - 1:], 'corr', forward_pairs)  3.04 us
  transfers between devices with their start and end apart: 2, of which 0 were waited for; matrix products, arithmetic and copies ran while one was open for 0% of the time, Pallas kernels for 0%

profile of v1, /device:TPU:0, one launch (start us, length us, event | category | flops | bytes accessed | tf_op | source)
XLA Modules:
  0.0 89.7 jit_solution(31640227416905348)
XLA Ops:
  0.6 0.0 copy-start.3
  0.6 1.0 %broadcast_in_dim.3.pix_ref = s32[1,23040]{1,0:T(1,128)S(1)} reshape(s32[23040]{0:T(1024)} %param.10) | data formatting | bytes 184320 | tf_op jit(solution)/shard_map/broadcast_in_dim | solution.py:200
  1.6 0.0 copy-done.3
  1.6 0.0 copy-start.2
  1.7 1.2 %copy-done.2 = bf16[8,256,256]{2,1,0:T(8,128)(2,1)S(1)} copy-done((bf16[8,256,256]{2,1,0:T(8,128)(2,1)S(1)}, bf16[8,256,256]{2,1,0:T(8,128)(2,1)}, u32[]{:S(2)}) %copy-start.2) | copy-done | bytes 1048600
  2.9 0.0 copy-start.4
  2.9 0.9 %copy-done.4 = bf16[256,512]{1,0:T(8,128)(2,1)S(1)} copy-done((bf16[256,512]{1,0:T(8,128)(2,1)S(1)}, bf16[256,512]{1,0:T(8,128)(2,1)}, u32[]{:S(2)}) %copy-start.4) | copy-done | bytes 262168
  3.8 0.0 copy-start.5
  3.8 0.9 %copy-done.5 = bf16[256,512]{1,0:T(8,128)(2,1)S(1)} copy-done((bf16[256,512]{1,0:T(8,128)(2,1)S(1)}, bf16[256,512]{1,0:T(8,128)(2,1)}, u32[]{:S(2)}) %copy-start.5) | copy-done | bytes 262168
  4.8 0.0 copy-start.6
  4.8 0.0 copy-start.1
  4.8 43.3 %shard_map.95.polar_ref = bf16[8,23040]{1,0:T(8,128)(2,1)S(1)} custom-call(bf16[8,256,256]{2,1,0:T(8,128)(2,1)S(1)} %copy-done.2, bf16[256,512]{1,0:T(8,128)(2,1)S(1)} %copy-done.5, bf16[256,512]{1,0:T(8,128)(2,1)S(1)} %copy-done.4, s32[1,23040]{1,0:T(1,128)S(1)} %broadcast_in_dim.3.pix_ref, f32[2,23040]{1,0:T(2,128)S(1)} %copy-done.3), custom_call_target="tpu_custom_call" | custom-call | flops 24159191040 | bytes 3145728 | tf_op jit(solution)/shard_map/pallas_call | solution.py:187
  48.0 0.0 copy-start
  48.1 0.1 fusion
  48.2 1.4 %collective-permute-start.1 = (bf16[1,23040]{1,0:T(2,128)(2,1)S(1)}, bf16[1,23040]{1,0:T(2,128)(2,1)S(1)}, u32[]{:S(2)}, u32[]{:S(2)}) collective-permute-start(bf16[1,23040]{1,0:T(2,128)(2,1)S(1)} %get-tuple-element.6), channel_id=1, source_target_pairs={{1,0},{2,1},{3,2},{4,3},{5,4},{6,5},{7,6},{8,7},{9,8},{10,9},{11,1... | collective-permute-start | bytes 138248 | tf_op jit(solution)/shard_map/ppermute | solution.py:204
  49.6 3.0 %collective-permute-start = (bf16[1,23040]{1,0:T(2,128)(2,1)S(1)}, bf16[1,23040]{1,0:T(2,128)(2,1)S(1)}, u32[]{:S(2)}, u32[]{:S(2)}) collective-permute-start(bf16[1,23040]{1,0:T(2,128)(2,1)S(1)} %get-tuple-element.7), channel_id=1, source_target_pairs={{0,1},{1,2},{2,3},{3,4},{4,5},{5,6},{6,7},{7,8},{8,9},{9,10},{10,1... | collective-permute-start | bytes 138248 | tf_op jit(solution)/shard_map/ppermute | solution.py:203
  52.7 0.0 copy-done.6
  52.7 0.3 reduce
  52.9 0.1 reshape.7
  53.1 25.3 %all_gather.3.templ_ref = bf16[1024,384]{1,0:T(8,128)(2,1)S(1)} all-gather(bf16[64,384]{1,0:T(8,128)(2,1)S(1)} %pad.4), channel_id=1, replica_groups=mesh['groups'=2,'corr'=16] {'corr'}, dimensions={0}, use_global_device_ids=true | all-gather | bytes 835584 | tf_op jit(solution)/shard_map/all_gather | solution.py:186
  78.4 0.0 collective-permute-done.1.high_ref
  78.4 0.0 collective-permute-done.low_ref
  78.4 0.0 copy-done.1
  78.4 0.0 copy-done
  78.4 10.7 %shard_map.96 = (bf16[8,23040]{1,0:T(8,128)(2,1)}, f32[8,128]{1,0:T(8,128)S(1)}) custom-call(bf16[8,23040]{1,0:T(8,128)(2,1)S(1)} %shard_map.95.polar_ref, bf16[1,23040]{1,0:T(2,128)(2,1)S(1)} %collective-permute-done.low_ref, bf16[1,23040]{1,0:T(2,128)(2,1)S(1)} %collective-permute-done.1.high_ref, bf16[1024,384]{1,0:T(8,128)(2,1)S(1)} %all_gather.3.templ_ref, ...), custom_call_target="tpu_custom_call" | custom-call | tf_op jit(solution)/shard_map/pallas_call | solution.py:206
  89.1 0.6 slice_reduce_fusion
  (1 shorter events, 0.0 us)
Async XLA Ops:
  0.6 1.0 %copy-start.3 = (f32[2,23040]{1,0:T(2,128)S(1)}, f32[2,23040]{1,0:T(2,128)}, u32[]{:S(2)}) copy-start(f32[2,23040]{1,0:T(2,128)} %frac_ref.1) | copy-start | bytes 552964
  1.6 1.2 %copy-start.2 = (bf16[8,256,256]{2,1,0:T(8,128)(2,1)S(1)}, bf16[8,256,256]{2,1,0:T(8,128)(2,1)}, u32[]{:S(2)}) copy-start(bf16[8,256,256]{2,1,0:T(8,128)(2,1)} %pat_ref.1) | copy-start | bytes 3145732
  2.9 0.9 %copy-start.4 = (bf16[256,512]{1,0:T(8,128)(2,1)S(1)}, bf16[256,512]{1,0:T(8,128)(2,1)}, u32[]{:S(2)}) copy-start(bf16[256,512]{1,0:T(8,128)(2,1)} %constant.12.clone.second_ref) | copy-start | bytes 786436
  3.8 0.9 %copy-start.5 = (bf16[256,512]{1,0:T(8,128)(2,1)S(1)}, bf16[256,512]{1,0:T(8,128)(2,1)}, u32[]{:S(2)}) copy-start(bf16[256,512]{1,0:T(8,128)(2,1)} %constant.11.clone.first_ref) | copy-start | bytes 786436
  4.8 47.9 %copy-start.6 = (bf16[1,23040]{1,0:T(2,128)(2,1)S(1)}, bf16[1,23040]{1,0:T(2,128)(2,1)}, u32[]{:S(2)}) copy-start(bf16[1,23040]{1,0:T(2,128)(2,1)} %param.9) | copy-start | bytes 138244
  4.8 73.6 %copy-start.1 = (bf16[384,1024]{1,0:T(8,128)(2,1)S(1)}, bf16[384,1024]{1,0:T(8,128)(2,1)}, u32[]{:S(2)}) copy-start(bf16[384,1024]{1,0:T(8,128)(2,1)} %constant.13.clone.fwd_ref) | copy-start | bytes 2359300
  48.0 30.3 %copy-start = (f32[512,384]{1,0:T(8,128)S(1)}, f32[512,384]{1,0:T(8,128)}, u32[]{:S(2)}) copy-start(f32[512,384]{1,0:T(8,128)} %constant.14.clone.inv_ref) | copy-start | bytes 2359300
  48.2 30.2 %collective-permute-start.1 = (bf16[1,23040]{1,0:T(2,128)(2,1)S(1)}, bf16[1,23040]{1,0:T(2,128)(2,1)S(1)}, u32[]{:S(2)}, u32[]{:S(2)}) collective-permute-start(bf16[1,23040]{1,0:T(2,128)(2,1)S(1)} %get-tuple-element.6), channel_id=1, source_target_pairs={{1,0},{2,1},{3,2},{4,3},{5,4},{6,5},{7,6},{8,7},{9,8},{10,9},{11,1... | collective-permute-start | bytes 138248 | tf_op jit(solution)/shard_map/ppermute | solution.py:204
  49.6 28.7 %collective-permute-start = (bf16[1,23040]{1,0:T(2,128)(2,1)S(1)}, bf16[1,23040]{1,0:T(2,128)(2,1)S(1)}, u32[]{:S(2)}, u32[]{:S(2)}) collective-permute-start(bf16[1,23040]{1,0:T(2,128)(2,1)S(1)} %get-tuple-element.7), channel_id=1, source_target_pairs={{0,1},{1,2},{2,3},{3,4},{4,5},{5,6},{6,7},{7,8},{8,9},{9,10},{10,1... | collective-permute-start | bytes 138248 | tf_op jit(solution)/shard_map/ppermute | solution.py:203

commit v2 on v1

v2 whole, which is shorter than its diff:
```python
import functools
import math

import jax
import jax.numpy as jnp
import ml_dtypes
import numpy as np
from jax import lax
from jax.experimental import pallas as pl
from jax.experimental.pallas import tpu as pltpu
from jax.sharding import PartitionSpec as P

RADII = 64
ANGLES = 360
FREQ = 181
SIGMA = 1.5
WIDE = 384
HALF = 256
CHUNK = 256
VMEM = pl.BlockSpec(memory_space=pltpu.VMEM)


def filter_tables(size):
    ids = np.arange(size)
    squared = ((ids[:, None] - ids[None, :]) ** 2).astype(np.float32)
    bell = np.exp(-squared / np.float32(2 * SIGMA**2)) / np.float32(math.sqrt(2 * math.pi) * SIGMA)
    curve = (squared / np.float32(SIGMA**4) - np.float32(1 / SIGMA**2)) * bell
    bell, curve = bell.astype(ml_dtypes.bfloat16), curve.astype(ml_dtypes.bfloat16)
    return np.concatenate([bell, curve], axis=1), np.concatenate([curve, bell], axis=1)


def split(table):
    high = table.astype(ml_dtypes.bfloat16)
    low = (table - high.astype(np.float64)).astype(ml_dtypes.bfloat16)
    return np.concatenate([high, low], axis=1)


def dft_tables():
    phase = np.outer(np.arange(ANGLES), np.arange(FREQ)) % ANGLES * (2 * math.pi / ANGLES)
    forward = np.zeros((WIDE, 2 * HALF))
    forward[:ANGLES, :FREQ] = np.cos(phase)
    forward[:ANGLES, HALF : HALF + FREQ] = -np.sin(phase)
    factor = np.full((FREQ, 1), 2.0 / ANGLES)
    factor[0] = factor[FREQ - 1] = 1.0 / ANGLES
    inverse = np.zeros((2 * HALF, WIDE))
    inverse[:FREQ, :ANGLES] = np.cos(phase).T * factor
    inverse[HALF : HALF + FREQ, :ANGLES] = -np.sin(phase).T * factor
    inverse[:, ANGLES:] = inverse[:, :1]
    return split(forward), inverse.astype(np.float32)


def pick_tree(get, masks, level, at):
    if level == 0:
        return get(at)
    low = pick_tree(get, masks, level - 1, at)
    high = pick_tree(get, masks, level - 1, at + (1 << (level - 1)))
    return jnp.where(masks[level - 1], high, low)


def column_weights(pix_ref, frac_ref, tile, side, out_ref):
    ids = lax.broadcasted_iota(jnp.int32, (side, 128), 0)
    for part in range(CHUNK // 128):
        col = pix_ref[pl.ds(tile + part, 1), :] & (side - 1)
        across = frac_ref[0, pl.ds(tile + part, 1), :]
        weights = jnp.where(ids == col, 1.0 - across, jnp.where(ids == col + 1, across, 0.0))
        out_ref[:, part * 128 : (part + 1) * 128] = weights.astype(jnp.bfloat16)


def sample_step(pix_ref, frac_ref, rows_ref, weights_ref, tile, count, bits):
    taken = jnp.dot(rows_ref[...], weights_ref[...], preferred_element_type=jnp.float32)
    out = []
    for part in range(CHUNK // 128):
        lanes = slice(part * 128, (part + 1) * 128)
        row = jnp.broadcast_to(pix_ref[pl.ds(tile + part, 1), :] >> (bits + 1), (count, 128))
        downward = jnp.broadcast_to(frac_ref[1, pl.ds(tile + part, 1), :], (count, 128))
        even_at, odd_at = (row + 1) >> 1, row >> 1
        even_masks = [(even_at & (1 << b)) != 0 for b in range(bits)]
        odd_masks = [(odd_at & (1 << b)) != 0 for b in range(bits)]

        def row_of(r):
            return taken[r * count : (r + 1) * count, lanes]

        even = pick_tree(lambda i: row_of(2 * i), even_masks, bits, 0)
        odd = pick_tree(lambda i: row_of(2 * i + 1), odd_masks, bits, 0)
        is_odd = (row & 1) != 0
        top = jnp.where(is_odd, odd, even)
        bottom = jnp.where(is_odd, even, odd)
        polar = (1.0 - downward) * top + downward * bottom
        out.append(polar.astype(jnp.bfloat16).astype(jnp.float32))
    return out


def kernel(
    size, pat_hbm, first_hbm, second_hbm, pix_hbm, frac_hbm, templ_hbm, fwd_hbm, inv_hbm,
    smooth_ref, best_ref,
    pat_ref, first_ref, second_ref, pix_ref, frac_ref, templ_ref, fwd_ref, inv_ref,
    wide_ref, rows_ref, even_ref, odd_ref, padded_ref, line_ref, spec_ref, templ_spec_ref,
    cross_ref, library_ref, last_ref, first_row_ref, low_ref, high_ref,
    load_sem, send_sem, recv_sem, halo_send, halo_recv,
):
    me = lax.axis_index("corr")
    loads = [
        pltpu.make_async_copy(source, target, load_sem.at[i])
        for i, (source, target) in enumerate((
            (templ_hbm, templ_ref), (pat_hbm, pat_ref), (first_hbm, first_ref),
            (second_hbm, second_ref), (pix_hbm, pix_ref), (frac_hbm, frac_ref),
            (fwd_hbm, fwd_ref), (inv_hbm, inv_ref),
        ))
    ]
    for load in loads:
        load.start()

    barrier = pltpu.get_barrier_semaphore()

    def partner(k):
        return {"corr": lax.rem(me + k, size)}

    @pl.loop(1, size)
    def _(k):
        pl.semaphore_signal(
            barrier, inc=1, device_id=partner(k), device_id_type=pl.DeviceIdType.MESH
        )

    pl.semaphore_wait(barrier, size - 1)
    loads[0].wait()

    def share(k):
        return pltpu.make_async_remote_copy(
            src_ref=templ_ref,
            dst_ref=library_ref.at[me],
            send_sem=send_sem.at[k],
            recv_sem=recv_sem.at[k],
            device_id=partner(k),
            device_id_type=pl.DeviceIdType.MESH,
        )

    @pl.loop(1, size)
    def _(k):
        share(k).start()

    library_ref[me] = templ_ref[...]

    count, side = pat_ref.shape[0], pat_ref.shape[1]
    bits = side.bit_length() - 2
    tiles = pix_ref.shape[0]
    width = tiles * 128
    for load in loads[1:4]:
        load.wait()
    for p in range(count):
        left = jnp.dot(pat_ref[p], first_ref[...], preferred_element_type=jnp.float32)
        left = left.astype(jnp.bfloat16)
        left = jnp.concatenate([left[:, :side], left[:, side:]], axis=0)
        filtered = jnp.dot(second_ref[...], left, preferred_element_type=jnp.float32)
        wide_ref[:, p, :] = filtered
    rows_ref[...] = wide_ref[...].reshape(side * count, side).astype(jnp.bfloat16)
    loads[4].wait()
    loads[5].wait()

    each = CHUNK // 128
    pairs = tiles // (2 * each)
    column_weights(pix_ref, frac_ref, 0, side, even_ref)

    def keep(tile, rows):
        for part, polar in enumerate(rows):
            padded_ref[tile + part] = polar
            first_row_ref[pl.ds(tile + part, 1), :] = polar[:1]
            last_ref[pl.ds(tile + part, 1), :] = polar[count - 1 :]

    @pl.loop(0, pairs)
    def _(step):
        now = step * (2 * each)
        later = lax.rem(step + 1, pairs) * (2 * each)
        column_weights(pix_ref, frac_ref, now + each, side, odd_ref)
        rows = sample_step(pix_ref, frac_ref, rows_ref, even_ref, now, count, bits)
        column_weights(pix_ref, frac_ref, later, side, even_ref)
        more = sample_step(pix_ref, frac_ref, rows_ref, odd_ref, now + each, count, bits)
        keep(now, rows)
        keep(now + each, more)

    def halo(i, source, target, to):
        return pltpu.make_async_remote_copy(
            src_ref=source,
            dst_ref=target,
            send_sem=halo_send.at[i],
            recv_sem=halo_recv.at[i],
            device_id={"corr": to},
            device_id_type=pl.DeviceIdType.MESH,
        )

    upward = halo(0, last_ref, low_ref, lax.rem(me + 1, size))
    downward = halo(1, first_row_ref, high_ref, lax.rem(me + size - 1, size))
    upward.start()
    downward.start()
    loads[6].wait()
    loads[7].wait()

    @pl.loop(1, size)
    def _(k):
        share(k).wait()

    def spectrum(lines):
        both = jnp.dot(lines, fwd_ref[...], preferred_element_type=jnp.float32)
        return both[:, : 2 * HALF] + both[:, 2 * HALF :]

    @pl.loop(0, size)
    def _(t):
        templ_spec_ref[pl.ds(pl.multiple_of(t * RADII, RADII), RADII), :] = spectrum(library_ref[t])

    upward.wait()
    downward.wait()
    has_low = jnp.where(me > 0, 1.0, 0.0)
    has_high = jnp.where(me < size - 1, 1.0, 0.0)
    ids = lax.broadcasted_iota(jnp.int32, (count, 128), 0)
    total = jnp.zeros((count, 128), jnp.float32)
    for tile in range(tiles):
        rows = padded_ref[tile]
        low = jnp.broadcast_to(low_ref[tile : tile + 1, :], rows.shape) * has_low
        high = jnp.broadcast_to(high_ref[tile : tile + 1, :], rows.shape) * has_high
        before = jnp.where(ids == 0, low, pltpu.roll(rows, 1, 0))
        after = jnp.where(ids == count - 1, high, pltpu.roll(rows, count - 1, 0))
        smooth = ((before + 2.0 * rows + after) * 0.25).astype(jnp.bfloat16)
        smooth_ref[:, tile * 128 : (tile + 1) * 128] = smooth
        smooth = smooth.astype(jnp.float32)
        padded_ref[tile] = smooth
        total = total + smooth * smooth
    pattern_norm = jnp.sqrt(jnp.sum(total, axis=1, keepdims=True) + 1e-06)

    real_lane = lax.broadcasted_iota(jnp.int32, (count, WIDE), 1) < ANGLES
    for r in range(RADII):
        start = r * ANGLES
        base = start // 128
        window = jnp.concatenate([padded_ref[min(base + i, tiles - 1)] for i in range(4)], axis=1)
        if start > base * 128:
            window = pltpu.roll(window, 512 - (start - base * 128), 1)
        line_ref[r * count : (r + 1) * count, :] = jnp.where(real_lane, window[:, :WIDE], 0.0)
    spec_ref[...] = spectrum(line_ref[...].astype(jnp.bfloat16))

    @pl.loop(0, size)
    def _(t):
        lines = library_ref[t].astype(jnp.float32)
        norm = jnp.sqrt(jnp.sum(lines * lines, keepdims=True) + 1e-06)
        real = jnp.zeros((count, HALF), jnp.float32)
        imag = jnp.zeros((count, HALF), jnp.float32)
        for r in range(RADII):
            pat = spec_ref[r * count : (r + 1) * count, :]
            tem = templ_spec_ref[pl.ds(t * RADII + r, 1), :]
            pr, pi, tr, ti = pat[:, :HALF], pat[:, HALF:], tem[:, :HALF], tem[:, HALF:]
            real = real + pr * tr + pi * ti
            imag = imag + pr * ti - pi * tr
        out = pl.ds(pl.multiple_of(t * count, count), count)
        scale = 1.0 / norm
        cross_ref[out, :HALF] = real * scale
        cross_ref[out, HALF:] = imag * scale

    scaled = jnp.dot(
        cross_ref[...], inv_ref[...], precision=lax.Precision.HIGHEST,
        preferred_element_type=jnp.float32,
    )
    top = jnp.max(scaled.reshape(size, count, WIDE), axis=0)
    best = jnp.max(top, axis=1, keepdims=True)
    best = best * math.sqrt(RADII * ANGLES) / pattern_norm
    best_ref[...] = jnp.broadcast_to(best, best_ref.shape)


def body(patterns, templates, pixels, fractions):
    count, side = patterns.shape[0], patterns.shape[1]
    width = pixels.shape[0]
    tiles = width // 128
    first, second = filter_tables(side)
    forward, inverse = dft_tables()
    size = lax.axis_size("corr")
    own = jnp.pad(templates.reshape(-1, ANGLES), ((0, 0), (0, WIDE - ANGLES)))
    operands = (
        patterns, jnp.asarray(first), jnp.asarray(second), pixels.reshape(tiles, 128),
        fractions.reshape(2, tiles, 128), own, jnp.asarray(forward), jnp.asarray(inverse),
    )
    f32, bf16 = jnp.float32, jnp.bfloat16
    smoothed, best = pl.pallas_call(
        functools.partial(kernel, size),
        out_shape=(
            jax.ShapeDtypeStruct((count, width), bf16),
            jax.ShapeDtypeStruct((count, 128), f32),
        ),
        in_specs=[pl.BlockSpec(memory_space=pl.ANY)] * 8,
        out_specs=(VMEM, VMEM),
        scratch_shapes=[pltpu.VMEM(x.shape, x.dtype) for x in operands]
        + [
            pltpu.VMEM((side, count, side), f32),
            pltpu.VMEM((side * count, side), bf16),
            pltpu.VMEM((side, CHUNK), bf16),
            pltpu.VMEM((side, CHUNK), bf16),
            pltpu.VMEM((tiles, count, 128), f32),
            pltpu.VMEM((RADII * count, WIDE), f32),
            pltpu.VMEM((RADII * count, 2 * HALF), f32),
            pltpu.VMEM((size * RADII, 2 * HALF), f32),
            pltpu.VMEM((size * count, 2 * HALF), f32),
            pltpu.VMEM((size, RADII, WIDE), bf16),
        ]
        + [pltpu.VMEM((tiles, 128), f32)] * 4
        + [
            pltpu.SemaphoreType.DMA((8,)),
            pltpu.SemaphoreType.DMA((size,)),
            pltpu.SemaphoreType.DMA((size,)),
            pltpu.SemaphoreType.DMA((2,)),
            pltpu.SemaphoreType.DMA((2,)),
        ],
        compiler_params=pltpu.CompilerParams(
            vmem_limit_bytes=56 << 20, collective_id=0, has_side_effects=True
        ),
        cost_estimate=pl.CostEstimate(
            flops=2 * count * side * side * width, bytes_accessed=4 << 20, transcendentals=0
        ),
    )(*operands)
    return smoothed, best[:, 0]


def solution(mesh):
    in_specs = (P(("groups", "corr"), None, None), P("corr", None), P(), P())
    out_specs = (P(("groups", "corr"), None), P(("groups", "corr")))
    return jax.shard_map(body, mesh=mesh, in_specs=in_specs, out_specs=out_specs, check_vma=False)
```

time: 90 us -> 61.2 us (0.68)
  blocking collectives: 25.3 us -> 0 us
  starting transfers between devices: 4.46 us -> 0 us
  other arithmetic: 0.26 us -> 1.18 us
    all_gather x1 -> x0, blocking collectives: 25.3 us -> none  [body(): library = lax.all_gather(own, 'corr', axis=0, tiled=True)]
    ppermute x2 -> x0, starting transfers between devices: 4.46 us -> none  [the longest x1 3.04 us: body(): low = lax.ppermute(polar[count - 1:], 'corr', forward_pairs)]
    unnamed x14 -> x3, local copies, waits for them, and re-layouts: 3.14 us -> 1.75 us
    broadcast_in_dim x1 -> x0, local copies, waits for them, and re-layouts: 0.99 us -> none  [body(): pixels[None]]
    unnamed x1, other arithmetic: 0.26 us -> 1.18 us
    pallas_call x2 -> x1, Pallas kernels: 54 us -> 54.5 us  [body(): pl.pallas_call(functools.partial(kernel, size), out_shape=(jax.ShapeDtype...]
  transfers between devices with their start and end apart: 2 -> 0, of which waited for: 0 -> 0; matrix products, arithmetic and copies ran while one was open for 0% -> 0% of each run, Pallas kernels for 0% -> 0%
where the time goes in v2:
time: 61.2 us; the launch traced here: 61 us
  Pallas kernels  54.5 us (89%)
  local copies, waits for them, and re-layouts  4.64 us (8%)
  other arithmetic  1.18 us (2%)
  between operations  0.65 us (1%)
    pallas_call x1, Pallas kernels, body(): pl.pallas_call(functools.partial(kernel, size), out_shape=(jax.ShapeDtype...  54.5 us
    unnamed x3, local copies, waits for them, and re-layouts  1.75 us
    slice x1, local copies, waits for them, and re-layouts, body(): return (smoothed, best[:, 0])  1.31 us

profile of v2, /device:TPU:0, one launch (start us, length us, event | category | flops | bytes accessed | tf_op | source)
XLA Modules:
  0.0 61.0 jit_solution(1238637599131589258)
XLA Ops:
  0.6 0.0 copy-start
  0.6 1.2 %reduce = bf16[23040]{0:T(1024)(128)(2,1)S(1)} reduce(bf16[1,23040]{1,0:T(2,128)(2,1)} %param.9, bf16[]{:T(256)} %constant.19), dimensions={0}, to_apply=%param.9.reduce_sub_computation | reduce | bytes 92162 | tf_op args[1]
  1.8 0.1 reshape.15
  2.0 0.6 %pad.4.templ_hbm = bf16[64,384]{1,0:T(8,128)(2,1)} pad(bf16[64,360]{1,0:T(8,128)(2,1)S(1)} %reshape.15, bf16[]{:T(256)} %constant.10.clone.1), padding=0_0x0_24 | pad | bytes 95234 | tf_op jit(solution)/shard_map/jit(_pad)/pad | solution.py:272
  2.6 0.0 copy-done
  2.6 0.8 %reshape.14.frac_hbm = f32[2,180,128]{2,1,0:T(8,128)} reshape(f32[2,23040]{1,0:T(2,128)S(1)} %copy-done) | data formatting | bytes 368640 | tf_op jit(solution)/shard_map/reshape | solution.py:275
  3.4 54.5 %shard_map.95 = (bf16[8,23040]{1,0:T(8,128)(2,1)}, f32[8,128]{1,0:T(8,128)}) custom-call(bf16[8,256,256]{2,1,0:T(8,128)(2,1)} %pat_hbm.1, bf16[256,512]{1,0:T(8,128)(2,1)} %constant.11.clone.first_hbm, bf16[256,512]{1,0:T(8,128)(2,1)} %constant.12.clone.second_hbm, s32[180,128]{1,0:T(8,128)} %bitcast.1, f32[2,180,128]{2,1,0:T(8,128)} %reshape.14.frac_hbm, ...), custom_call_target="tpu_custom_call" | custom-call | flops 24159191040 | bytes 4194304 | tf_op jit(solution)/shard_map/pallas_call | solution.py:278
  58.0 1.3 %slice_reduce_fusion = f32[8]{0:T(128)} fusion(f32[8,128]{1,0:T(8,128)} %get-tuple-element.5), kind=kLoop, calls=%fused_computation | loop fusion | bytes 64 | tf_op jit(solution)/shard_map/slice | solution.py:314
  59.3 1.7 %copy.11 = bf16[8,23040]{1,0:T(8,128)(2,1)} copy(bf16[8,23040]{1,0:T(8,128)(2,1)} %get-tuple-element.8) | data formatting | bytes 737280
Async XLA Ops:
  0.6 2.0 %copy-start = (f32[2,23040]{1,0:T(2,128)S(1)}, f32[2,23040]{1,0:T(2,128)}, u32[]{:S(2)}) copy-start(f32[2,23040]{1,0:T(2,128)} %param.11) | copy-start | bytes 552964

commit v3 on v2

--- a/solution.py
+++ b/solution.py
@@ -16,7 +16,8 @@
 SIGMA = 1.5
 WIDE = 384
 HALF = 256
-CHUNK = 256
+CHUNK = 768
+GROUP = 4
 VMEM = pl.BlockSpec(memory_space=pltpu.VMEM)
 
 
@@ -27,12 +28,6 @@
     curve = (squared / np.float32(SIGMA**4) - np.float32(1 / SIGMA**2)) * bell
     bell, curve = bell.astype(ml_dtypes.bfloat16), curve.astype(ml_dtypes.bfloat16)
     return np.concatenate([bell, curve], axis=1), np.concatenate([curve, bell], axis=1)
-
-
-def split(table):
-    high = table.astype(ml_dtypes.bfloat16)
-    low = (table - high.astype(np.float64)).astype(ml_dtypes.bfloat16)
-    return np.concatenate([high, low], axis=1)
 
 
 def dft_tables():
@@ -46,7 +41,7 @@
     inverse[:FREQ, :ANGLES] = np.cos(phase).T * factor
     inverse[HALF : HALF + FREQ, :ANGLES] = -np.sin(phase).T * factor
     inverse[:, ANGLES:] = inverse[:, :1]
-    return split(forward), inverse.astype(np.float32)
+    return forward.astype(ml_dtypes.bfloat16), inverse.astype(ml_dtypes.bfloat16)
 
 
 def pick_tree(get, masks, level, at):
@@ -57,11 +52,15 @@
     return jnp.where(masks[level - 1], high, low)
 
 
+def lanes_of(tile):
+    return pl.ds(pl.multiple_of(tile * 128, 128), 128)
+
+
 def column_weights(pix_ref, frac_ref, tile, side, out_ref):
     ids = lax.broadcasted_iota(jnp.int32, (side, 128), 0)
     for part in range(CHUNK // 128):
         col = pix_ref[pl.ds(tile + part, 1), :] & (side - 1)
-        across = frac_ref[0, pl.ds(tile + part, 1), :]
+        across = frac_ref[0:1, lanes_of(tile + part)]
         weights = jnp.where(ids == col, 1.0 - across, jnp.where(ids == col + 1, across, 0.0))
         out_ref[:, part * 128 : (part + 1) * 128] = weights.astype(jnp.bfloat16)
 
@@ -72,7 +71,7 @@
     for part in range(CHUNK // 128):
         lanes = slice(part * 128, (part + 1) * 128)
         row = jnp.broadcast_to(pix_ref[pl.ds(tile + part, 1), :] >> (bits + 1), (count, 128))
-        downward = jnp.broadcast_to(frac_ref[1, pl.ds(tile + part, 1), :], (count, 128))
+        downward = jnp.broadcast_to(frac_ref[1:2, lanes_of(tile + part)], (count, 128))
         even_at, odd_at = (row + 1) >> 1, row >> 1
         even_masks = [(even_at & (1 << b)) != 0 for b in range(bits)]
         odd_masks = [(odd_at & (1 << b)) != 0 for b in range(bits)]
@@ -93,8 +92,8 @@
 def kernel(
     size, pat_hbm, first_hbm, second_hbm, pix_hbm, frac_hbm, templ_hbm, fwd_hbm, inv_hbm,
     smooth_ref, best_ref,
-    pat_ref, first_ref, second_ref, pix_ref, frac_ref, templ_ref, fwd_ref, inv_ref,
-    wide_ref, rows_ref, even_ref, odd_ref, padded_ref, line_ref, spec_ref, templ_spec_ref,
+    pat_ref, first_ref, second_ref, pix_ref, frac_ref, row_ref, fwd_ref, inv_ref,
+    templ_ref, norm_ref, wide_ref, rows_ref, even_ref, odd_ref, padded_ref, line_ref, spec_ref, templ_spec_ref,
     cross_ref, library_ref, last_ref, first_row_ref, low_ref, high_ref,
     load_sem, send_sem, recv_sem, halo_send, halo_recv,
 ):
@@ -102,7 +101,7 @@
     loads = [
         pltpu.make_async_copy(source, target, load_sem.at[i])
         for i, (source, target) in enumerate((
-            (templ_hbm, templ_ref), (pat_hbm, pat_ref), (first_hbm, first_ref),
+            (templ_hbm, row_ref), (pat_hbm, pat_ref), (first_hbm, first_ref),
             (second_hbm, second_ref), (pix_hbm, pix_ref), (frac_hbm, frac_ref),
             (fwd_hbm, fwd_ref), (inv_hbm, inv_ref),
         ))
@@ -120,9 +119,6 @@
         pl.semaphore_signal(
             barrier, inc=1, device_id=partner(k), device_id_type=pl.DeviceIdType.MESH
         )
-
-    pl.semaphore_wait(barrier, size - 1)
-    loads[0].wait()
 
     def share(k):
         return pltpu.make_async_remote_copy(
@@ -133,12 +129,6 @@
             device_id=partner(k),
             device_id_type=pl.DeviceIdType.MESH,
         )
-
-    @pl.loop(1, size)
-    def _(k):
-        share(k).start()
-
-    library_ref[me] = templ_ref[...]
 
     count, side = pat_ref.shape[0], pat_ref.shape[1]
     bits = side.bit_length() - 2
@@ -153,6 +143,25 @@
         filtered = jnp.dot(second_ref[...], left, preferred_element_type=jnp.float32)
         wide_ref[:, p, :] = filtered
     rows_ref[...] = wide_ref[...].reshape(side * count, side).astype(jnp.bfloat16)
+    loads[0].wait()
+    real_lane = lax.broadcasted_iota(jnp.int32, (1, WIDE), 1) < ANGLES
+    row = row_ref[...].astype(jnp.float32)
+    for r in range(RADII):
+        start = r * ANGLES
+        base = min(start // 128, tiles - 4)
+        window = row[:, base * 128 : base * 128 + 512]
+        if start > base * 128:
+            window = pltpu.roll(window, 512 - (start - base * 128), 1)
+        line_ref[r : r + 1, :] = jnp.where(real_lane, window[:, :WIDE], 0.0)
+    templ_ref[...] = line_ref[0:RADII, :].astype(jnp.bfloat16)
+    pl.semaphore_wait(barrier, size - 1)
+
+    @pl.loop(1, size)
+    def _(k):
+        share(k).start()
+
+    library_ref[me] = templ_ref[...]
+
     loads[4].wait()
     loads[5].wait()
 
@@ -199,12 +208,20 @@
         share(k).wait()
 
     def spectrum(lines):
-        both = jnp.dot(lines, fwd_ref[...], preferred_element_type=jnp.float32)
-        return both[:, : 2 * HALF] + both[:, 2 * HALF :]
-
-    @pl.loop(0, size)
-    def _(t):
-        templ_spec_ref[pl.ds(pl.multiple_of(t * RADII, RADII), RADII), :] = spectrum(library_ref[t])
+        return jnp.dot(lines, fwd_ref[...], preferred_element_type=jnp.float32)
+
+    @pl.loop(0, size // GROUP)
+    def _(group):
+        lines = library_ref[pl.ds(group * GROUP, GROUP)].reshape(GROUP * RADII, WIDE)
+        at = pl.ds(pl.multiple_of(group * (GROUP * RADII), GROUP * RADII), GROUP * RADII)
+        templ_spec_ref[at, :] = spectrum(lines)
+        lines = lines.astype(jnp.float32)
+        squares = lines * lines
+        squares = squares[:, :128] + squares[:, 128:256] + squares[:, 256:]
+        for i in range(GROUP):
+            part = jnp.sum(squares[i * RADII : (i + 1) * RADII], axis=0, keepdims=True)
+            out = pl.ds(pl.multiple_of((group * GROUP + i) * count, count), count)
+            norm_ref[out, :] = jnp.broadcast_to(part, (count, 128))
 
     upward.wait()
     downward.wait()
@@ -235,31 +252,33 @@
         line_ref[r * count : (r + 1) * count, :] = jnp.where(real_lane, window[:, :WIDE], 0.0)
     spec_ref[...] = spectrum(line_ref[...].astype(jnp.bfloat16))
 
-    @pl.loop(0, size)
-    def _(t):
-        lines = library_ref[t].astype(jnp.float32)
-        norm = jnp.sqrt(jnp.sum(lines * lines, keepdims=True) + 1e-06)
-        real = jnp.zeros((count, HALF), jnp.float32)
-        imag = jnp.zeros((count, HALF), jnp.float32)
+    @pl.loop(0, size // GROUP)
+    def _(group):
+        zero = jnp.zeros((count, HALF), jnp.float32)
+        real, imag = [zero] * GROUP, [zero] * GROUP
         for r in range(RADII):
             pat = spec_ref[r * count : (r + 1) * count, :]
-            tem = templ_spec_ref[pl.ds(t * RADII + r, 1), :]
-            pr, pi, tr, ti = pat[:, :HALF], pat[:, HALF:], tem[:, :HALF], tem[:, HALF:]
-            real = real + pr * tr + pi * ti
-            imag = imag + pr * ti - pi * tr
-        out = pl.ds(pl.multiple_of(t * count, count), count)
-        scale = 1.0 / norm
-        cross_ref[out, :HALF] = real * scale
-        cross_ref[out, HALF:] = imag * scale
-
-    scaled = jnp.dot(
-        cross_ref[...], inv_ref[...], precision=lax.Precision.HIGHEST,
-        preferred_element_type=jnp.float32,
+            pr, pi = pat[:, :HALF], pat[:, HALF:]
+            for i in range(GROUP):
+                tem = templ_spec_ref[pl.ds((group * GROUP + i) * RADII + r, 1), :]
+                tr, ti = tem[:, :HALF], tem[:, HALF:]
+                real[i] = real[i] + pr * tr + pi * ti
+                imag[i] = imag[i] + pr * ti - pi * tr
+        for i in range(GROUP):
+            out = pl.ds(pl.multiple_of((group * GROUP + i) * count, count), count)
+            cross_ref[out, :HALF] = real[i]
+            cross_ref[out, HALF:] = imag[i]
+
+    shifted = jnp.dot(
+        cross_ref[...].astype(jnp.bfloat16), inv_ref[...], preferred_element_type=jnp.float32
     )
-    top = jnp.max(scaled.reshape(size, count, WIDE), axis=0)
-    best = jnp.max(top, axis=1, keepdims=True)
-    best = best * math.sqrt(RADII * ANGLES) / pattern_norm
-    best_ref[...] = jnp.broadcast_to(best, best_ref.shape)
+    shifted = jnp.maximum(jnp.maximum(shifted[:, :128], shifted[:, 128:256]), shifted[:, 256:])
+    norm = jnp.sqrt(jnp.sum(norm_ref[...], axis=1, keepdims=True) + 1e-06)
+    scaled = jnp.max(shifted, axis=1, keepdims=True) / norm
+    scaled = jnp.broadcast_to(scaled, (size * count, 128)).reshape(size, count, 128)
+    best = jnp.max(scaled, axis=0) * math.sqrt(RADII * ANGLES) / pattern_norm
+    diagonal = ids == lax.broadcasted_iota(jnp.int32, (count, 128), 1)
+    best_ref[...] = jnp.sum(jnp.where(diagonal, best, 0.0), axis=0, keepdims=True)[:, :count]
 
 
 def body(patterns, templates, pixels, fractions):
@@ -269,22 +288,23 @@
     first, second = filter_tables(side)
     forward, inverse = dft_tables()
     size = lax.axis_size("corr")
-    own = jnp.pad(templates.reshape(-1, ANGLES), ((0, 0), (0, WIDE - ANGLES)))
     operands = (
         patterns, jnp.asarray(first), jnp.asarray(second), pixels.reshape(tiles, 128),
-        fractions.reshape(2, tiles, 128), own, jnp.asarray(forward), jnp.asarray(inverse),
+        fractions, templates, jnp.asarray(forward), jnp.asarray(inverse),
     )
     f32, bf16 = jnp.float32, jnp.bfloat16
     smoothed, best = pl.pallas_call(
         functools.partial(kernel, size),
         out_shape=(
             jax.ShapeDtypeStruct((count, width), bf16),
-            jax.ShapeDtypeStruct((count, 128), f32),
+            jax.ShapeDtypeStruct((1, count), f32),
         ),
         in_specs=[pl.BlockSpec(memory_space=pl.ANY)] * 8,
         out_specs=(VMEM, VMEM),
         scratch_shapes=[pltpu.VMEM(x.shape, x.dtype) for x in operands]
         + [
+            pltpu.VMEM((RADII, WIDE), bf16),
+            pltpu.VMEM((size * count, 128), f32),
             pltpu.VMEM((side, count, side), f32),
             pltpu.VMEM((side * count, side), bf16),
             pltpu.VMEM((side, CHUNK), bf16),
@@ -311,7 +331,7 @@
             flops=2 * count * side * side * width, bytes_accessed=4 << 20, transcendentals=0
         ),
     )(*operands)
-    return smoothed, best[:, 0]
+    return smoothed, best.reshape(count)
 
 
 def solution(mesh):

time: 61.2 us -> 52.4 us (0.86)
  Pallas kernels: 54.5 us -> 49.4 us
  local copies, waits for them, and re-layouts: 4.64 us -> 2.27 us
  other arithmetic: 1.18 us -> 0 us
    pallas_call x1, Pallas kernels: 54.5 us -> 49.4 us  [body(): pl.pallas_call(functools.partial(kernel, size), out_shape=(jax.ShapeDtype...]
    slice x1 -> x0, local copies, waits for them, and re-layouts: 1.31 us -> none  [body(): return (smoothed, best[:, 0])]
    unnamed x1 -> x0, other arithmetic: 1.18 us -> none
    reshape x2 -> x0, local copies, waits for them, and re-layouts: 0.97 us -> none  [the longest x1 0.82 us: body(): fractions.reshape(2, tiles, 128)]
    pad x1 -> x0, local copies, waits for them, and re-layouts: 0.61 us -> none  [body(): own = jnp.pad(templates.reshape(-1, ANGLES), ((0, 0), (0, WIDE - ANGLES)))]
    unnamed x3 -> x4, local copies, waits for them, and re-layouts: 1.75 us -> 2.27 us
where the time goes in v3:
time: 52.4 us; the launch traced here: 52.3 us
  Pallas kernels  49.4 us (94%)
  local copies, waits for them, and re-layouts  2.27 us (4%)
  between operations  0.65 us (1%)
    pallas_call x1, Pallas kernels, body(): pl.pallas_call(functools.partial(kernel, size), out_shape=(jax.ShapeDtype...  49.4 us
    unnamed x4, local copies, waits for them, and re-layouts  2.27 us

profile of v3, /device:TPU:0, one launch (start us, length us, event | category | flops | bytes accessed | tf_op | source)
XLA Modules:
  0.0 52.3 jit_solution(14306553375555689617)
XLA Ops:
  0.6 49.4 %shard_map.95 = (bf16[8,23040]{1,0:T(8,128)(2,1)}, f32[1,8]{1,0:T(1,128)}) custom-call(bf16[8,256,256]{2,1,0:T(8,128)(2,1)} %pat_hbm.1, bf16[256,512]{1,0:T(8,128)(2,1)} %constant.8.clone.first_hbm, bf16[256,512]{1,0:T(8,128)(2,1)} %constant.9.clone.second_hbm, s32[180,128]{1,0:T(8,128)} %bitcast.2, f32[2,23040]{1,0:T(2,128)} %frac_hbm.1, ...), custom_call_target="tpu_custom_call" | custom-call | flops 24159191040 | bytes 4194304 | tf_op jit(solution)/shard_map/pallas_call | solution.py:296
  50.0 0.0 copy-start
  50.0 1.7 %copy.12 = bf16[8,23040]{1,0:T(8,128)(2,1)} copy(bf16[8,23040]{1,0:T(8,128)(2,1)} %get-tuple-element.8) | data formatting | bytes 737280
  51.8 0.0 copy-done
  51.8 0.5 copy.13
Async XLA Ops:
  50.0 1.8 %copy-start = (f32[1,8]{1,0:T(1,128)S(1)}, f32[1,8]{1,0:T(1,128)}, u32[]{:S(2)}) copy-start(f32[1,8]{1,0:T(1,128)} %get-tuple-element.5) | copy-start | bytes 100

commit v4 on v3

--- a/solution.py
+++ b/solution.py
@@ -16,7 +16,7 @@
 SIGMA = 1.5
 WIDE = 384
 HALF = 256
-CHUNK = 768
+CHUNK = 1280
 GROUP = 4
 VMEM = pl.BlockSpec(memory_space=pltpu.VMEM)
 
@@ -66,7 +66,17 @@
 
 
 def sample_step(pix_ref, frac_ref, rows_ref, weights_ref, tile, count, bits):
-    taken = jnp.dot(rows_ref[...], weights_ref[...], preferred_element_type=jnp.float32)
+    block = rows_ref.shape[0] // count
+    taken = jnp.concatenate(
+        [
+            jnp.dot(
+                rows_ref[i * block : (i + 1) * block, :], weights_ref[...],
+                preferred_element_type=jnp.float32,
+            )
+            for i in range(count)
+        ],
+        axis=0,
+    )
     out = []
     for part in range(CHUNK // 128):
         lanes = slice(part * 128, (part + 1) * 128)

time: 52.4 us -> 51.2 us (0.977)
  Pallas kernels: 49.4 us -> 48.1 us
    pallas_call x1, Pallas kernels: 49.4 us -> 48.1 us  [body(): pl.pallas_call(functools.partial(kernel, size), out_shape=(jax.ShapeDtype...]
where the time goes in v4:
time: 51.2 us; the launch traced here: 51 us
  Pallas kernels  48.1 us (94%)
  local copies, waits for them, and re-layouts  2.27 us (4%)
  between operations  0.65 us (1%)
    pallas_call x1, Pallas kernels, body(): pl.pallas_call(functools.partial(kernel, size), out_shape=(jax.ShapeDtype...  48.1 us
    unnamed x4, local copies, waits for them, and re-layouts  2.27 us

profile of v4, /device:TPU:0, one launch (start us, length us, event | category | flops | bytes accessed | tf_op | source)
XLA Modules:
  0.0 51.0 jit_solution(7776462634025051131)
XLA Ops:
  0.6 48.1 %shard_map.95 = (bf16[8,23040]{1,0:T(8,128)(2,1)}, f32[1,8]{1,0:T(1,128)}) custom-call(bf16[8,256,256]{2,1,0:T(8,128)(2,1)} %pat_hbm.1, bf16[256,512]{1,0:T(8,128)(2,1)} %constant.8.clone.first_hbm, bf16[256,512]{1,0:T(8,128)(2,1)} %constant.9.clone.second_hbm, s32[180,128]{1,0:T(8,128)} %bitcast.2, f32[2,23040]{1,0:T(2,128)} %frac_hbm.1, ...), custom_call_target="tpu_custom_call" | custom-call | flops 24159191040 | bytes 4194304 | tf_op jit(solution)/shard_map/pallas_call | solution.py:306
  48.8 0.0 copy-start
  48.8 1.7 %copy.12 = bf16[8,23040]{1,0:T(8,128)(2,1)} copy(bf16[8,23040]{1,0:T(8,128)(2,1)} %get-tuple-element.8) | data formatting | bytes 737280
  50.5 0.0 copy-done
  50.5 0.5 %copy.13 = f32[8]{0:T(128)} copy(f32[8]{0:T(128)S(1)} %bitcast.3) | data formatting | bytes 64
Async XLA Ops:
  48.8 1.8 %copy-start = (f32[1,8]{1,0:T(1,128)S(1)}, f32[1,8]{1,0:T(1,128)}, u32[]{:S(2)}) copy-start(f32[1,8]{1,0:T(1,128)} %get-tuple-element.5) | copy-start | bytes 100
